TPU v7x, 32 devices: a whole 2x2x4 slice. The times are simulated.
32 devices in a mesh: rep: 2 (over x), node: 2 (over core), dev: 8 (over z, y).
Axes of the slice: x: 2, y: 2, z: 4, core: 2. Of those that a mesh axis runs over, the one named last changes fastest.
Arguments:
- tokens: bfloat16 [1024, 7168], P(('rep', 'node', 'dev')), parts along dimension 0, may hold values from -6 to 6
- expert_picks: int32 [1024, 2], P(('rep', 'node', 'dev')), parts along dimension 0, may hold values from 0 to 3, all different within a row; in each aligned block of 32 rows (0 to 31, 32 to 63, ...) at most 32 rows name the same one
- mix_weights: float32 [1024, 2], P(('rep', 'node', 'dev')), parts along dimension 0, may hold values from 0.2 to 1
- w_gate: bfloat16 [7168, 4096], P(None, ('node', 'dev')), may hold values from -0.0625 to 0.0625
- w_up: bfloat16 [7168, 4096], P(None, ('node', 'dev')), may hold values from -0.0625 to 0.0625
- w_down: bfloat16 [4096, 7168], P(('node', 'dev')), may hold values from -0.1875 to 0.1875
Outputs:
- mixed: bfloat16 [1024, 7168], P(('rep', 'node', 'dev')), parts along dimension 0
There are 2 independent parts, one for each index of `rep`. A program takes and returns all parts, laid end to end along the dimension named above; an argument that names none is the same for every part. Nothing has to cross between parts.
Inputs may be any that keep to these rules, and one draw needn't show every extreme that they name: `expert_picks`: A row's 2 picks name different experts; in each aligned block of 32 rows (the rows of one device) no expert is named by more than 32 rows, a bound that some block reaches.
All inputs are finite; a program needn't handle non-finite values.
Results may differ from a plain program's by a relative error of at most 0.0064.
Values may be sent and summed in bfloat16 or wider, within the bound.
A program may use at most 128 MiB of HBM per device.

v0:
```python
import jax
import jax.numpy as jnp
from jax import lax
from jax.sharding import PartitionSpec as P

SHARDS = 4


def on_device(tokens, expert_picks, mix_weights, w_gate, w_up, w_down):
    rows_here = tokens.shape[0]
    model_width = tokens.shape[1]
    pick_count = expert_picks.shape[1]
    node_count = lax.axis_size("node")
    dev_count = lax.axis_size("dev")
    sources = node_count * dev_count
    experts = sources // SHARDS
    capacity = 2 * rows_here * pick_count // experts
    picks_flat = expert_picks.reshape(-1)
    onehot = (picks_flat[:, None] == jnp.arange(experts, dtype=jnp.int32)[None, :]).astype(
        jnp.int32
    )
    ranking = jnp.cumsum(onehot, axis=0) - onehot
    position = jnp.sum(ranking * onehot, axis=1)
    slot_index = picks_flat * capacity + position
    repeated = jnp.repeat(tokens, pick_count, axis=0)
    outgoing = (
        jnp.zeros((experts * capacity, model_width), jnp.bfloat16).at[slot_index].set(repeated)
    )
    spread = jnp.broadcast_to(
        outgoing.reshape(experts, 1, capacity, model_width),
        (experts, SHARDS, capacity, model_width),
    ).reshape(sources, capacity, model_width)
    incoming = lax.all_to_all(spread, ("node", "dev"), split_axis=0, concat_axis=0, tiled=True)
    leading = incoming.shape[0]
    row_count = incoming.shape[1]
    rows_in = incoming.reshape(leading * row_count, model_width)
    gate_proj = jnp.dot(rows_in, w_gate, preferred_element_type=jnp.float32)
    up_proj = jnp.dot(rows_in, w_up, preferred_element_type=jnp.float32)
    hidden = (jax.nn.silu(gate_proj) * up_proj).astype(jnp.bfloat16)
    shard_out = jnp.dot(hidden, w_down, preferred_element_type=jnp.float32).astype(jnp.bfloat16)
    returned = lax.all_to_all(
        shard_out.reshape(leading, row_count, model_width),
        ("node", "dev"),
        split_axis=0,
        concat_axis=0,
        tiled=True,
    )
    summed = jnp.sum(
        returned.reshape(experts, SHARDS, capacity, model_width).astype(jnp.float32), axis=1
    )
    expert_out = summed.astype(jnp.bfloat16).reshape(experts * capacity, model_width)
    picked = expert_out[slot_index].astype(jnp.float32).reshape(rows_here, pick_count, model_width)
    weighted = picked * mix_weights[:, :, None]
    return jnp.sum(weighted, axis=1).astype(jnp.bfloat16)


def solution(mesh):
    placed = (
        P(("rep", "node", "dev"), None),
        P(("rep", "node", "dev"), None),
        P(("rep", "node", "dev"), None),
        P(None, ("node", "dev")),
        P(None, ("node", "dev")),
        P(("node", "dev"), None),
    )
    return jax.shard_map(
        on_device,
        mesh=mesh,
        in_specs=placed,
        out_specs=P(("rep", "node", "dev"), None),
        check_vma=False,
    )
```

profile of v0, /device:TPU:0, one launch (start us, length us, event | category | flops | bytes accessed | tf_op | source)
XLA Modules:
  0.0 365.5 jit_solution(14797967985469675778)
XLA Ops:
  0.0 0.8 copy.11
  0.8 0.7 broadcast_multiply_fusion
  1.4 0.1 eq.15
  1.5 0.1 fusion.9
  1.6 0.1 reduce_window_sum.11
  1.7 0.2 select_reduce_fusion
  1.9 0.1 copy.10
  2.0 0.1 mul.36
  2.1 1.5 broadcast_in_dim.18
  3.6 0.3 reshape.74
  4.0 2.4 scatter_custom_fusion
  6.4 0.9 broadcast_in_dim.20
  7.3 0.0 copy-start.2
  7.3 169.3 %all_to_all.10 = bf16[16,32,7168]{2,1,0:T(8,128)(2,1)S(1)} all-to-all(bf16[16,32,7168]{2,1,0:T(8,128)(2,1)S(1)} %bitcast.22), channel_id=1, replica_groups=mesh['rep'=2,'node'=2,'dev'=8] {'node','dev'}, dimensions={0} | all-to-all | bytes 14680064 | tf_op jit(solution)/shard_map/all_to_all | solution.py:33
  176.6 0.0 copy-start
  176.6 3.0 copy-done
  179.7 0.0 copy-done.2
  179.7 2.1 fusion.12
  181.8 16.0 %convolution_convert_fusion = bf16[512,7168]{1,0:T(8,128)(2,1)} fusion(bf16[256,7168]{1,0:T(8,128)(2,1)} %param.11, bf16[512,7168]{1,0:T(8,128)(2,1)} %bitcast.21, bf16[7168,256]{1,0:T(8,128)(2,1)} %param.10, f32[512,256]{1,0:T(8,128)S(1)} %fusion.12), kind=kOutput, calls=%fused_computation.2 | convolution fusion | flops 3762552832 | bytes 22544384 | tf_op jit(solution)/shard_map/dot_general | solution.py:40
  197.7 0.0 copy-start.1
  197.7 5.0 %all-to-all-start.1 = ((bf16[16,32,7168]{2,1,0:T(8,128)(2,1)}), bf16[16,32,7168]{2,1,0:T(8,128)(2,1)}, u32[]{:S(2)}, u32[]{:S(2)}) async-start(bf16[16,32,7168]{2,1,0:T(8,128)(2,1)} %bitcast.19), calls=%async_computation.1 | async-start | bytes 14680064 | tf_op jit(solution)/shard_map/all_to_all | solution.py:41
  202.7 0.0 copy-done.1
  202.7 0.1 copy.12
  202.8 152.6 %all-to-all-done.1 = bf16[16,32,7168]{2,1,0:T(8,128)(2,1)} async-done(((bf16[16,32,7168]{2,1,0:T(8,128)(2,1)}), bf16[16,32,7168]{2,1,0:T(8,128)(2,1)}, u32[]{:S(2)}, u32[]{:S(2)}) %all-to-all-start.1) | async-done | bytes 7340064 | tf_op jit(solution)/shard_map/all_to_all | solution.py:41
  355.4 4.6 %bitcast_reduce_fusion = bf16[4,32,7168]{2,1,0:T(8,128)(2,1)S(1)} fusion(bf16[16,32,7168]{2,1,0:T(8,128)(2,1)} %all-to-all-done.1), kind=kLoop, calls=%fused_computation.3 | loop fusion | flops 2752512 | bytes 9175040 | tf_op jit(solution)/shard_map/reduce_sum | solution.py:48
  360.1 1.1 gather_fusion
  361.2 1.1 reshape.61
  362.3 3.2 multiply_reduce_fusion
  (2 shorter events, 0.0 us)
Async XLA Ops:
  7.3 172.4 %copy-start.2 = (bf16[7168,256]{1,0:T(8,128)(2,1)S(1)}, bf16[7168,256]{1,0:T(8,128)(2,1)}, u32[]{:S(2)}) copy-start(bf16[7168,256]{1,0:T(8,128)(2,1)} %param.9) | copy-start | bytes 11010052
  176.6 3.0 copy-start
  197.7 5.0 %copy-start.1 = (f32[32,2]{0,1:T(2,128)S(1)}, f32[32,2]{0,1:T(2,128)}, u32[]{:S(2)}) copy-start(f32[32,2]{0,1:T(2,128)} %param.8) | copy-start | bytes 772
  197.7 157.7 %all-to-all-start.1 = ((bf16[16,32,7168]{2,1,0:T(8,128)(2,1)}), bf16[16,32,7168]{2,1,0:T(8,128)(2,1)}, u32[]{:S(2)}, u32[]{:S(2)}) async-start(bf16[16,32,7168]{2,1,0:T(8,128)(2,1)} %bitcast.19), calls=%async_computation.1 | async-start | bytes 14680064 | tf_op jit(solution)/shard_map/all_to_all | solution.py:41
where the time goes:
time: 373 us; the launch traced here: 366 us
  blocking collectives  169 us (45%)
  waiting for transfers between devices  153 us (41%)
  matrix products  18.1 us (5%)
  local copies, waits for them, and re-layouts  11.6 us (3%)
  other arithmetic  8.85 us (2%)
  starting transfers between devices  4.99 us (1%)
    all_to_all x1, blocking collectives, on_device(): lax.all_to_all(spread, ('node', 'dev'), split_axis=0, concat_axis=0, tile...  169 us
    all_to_all x1, waiting for transfers between devices, on_device(): lax.all_to_all(shard_out.reshape(leading, row_count, model_width), ('node...  153 us
    dot_general x1, matrix products, on_device(): jnp.dot(hidden, w_down, preferred_element_type=jnp.float32)  16 us
  transfers between devices with their start and end apart: 1, of which 1 were waited for; matrix products, arithmetic and copies ran while one was open for 0% of the time, Pallas kernels for 0%

commit v1 on v0

--- a/solution.py
+++ b/solution.py
@@ -1,12 +1,287 @@
+import functools
+
 import jax
 import jax.numpy as jnp
 from jax import lax
+from jax.experimental import pallas as pl
+from jax.experimental.pallas import tpu as pltpu
 from jax.sharding import PartitionSpec as P
 
 SHARDS = 4
-
-
-def on_device(tokens, expert_picks, mix_weights, w_gate, w_up, w_down):
+LANES = 128
+MESH = pl.DeviceIdType.MESH
+CW, CCW = 0, 1
+
+
+def ring_kernel(
+    chips,
+    rows,
+    width,
+    picks_ref,
+    mix_ref,
+    tokens_ref,
+    gate_ref,
+    up_ref,
+    down_ref,
+    out_ref,
+    tok,
+    w_gate,
+    w_up,
+    w_down,
+    part,
+    sib_part,
+    sent,
+    got,
+    load_sem,
+    ag_send,
+    ag_recv,
+    sib_send,
+    sib_recv,
+    part_send,
+    part_recv,
+    rs_send,
+    rs_recv,
+):
+    half_ring = chips // 2
+    half = rows // 2
+    rep, node, dev = (lax.axis_index(a) for a in ("rep", "node", "dev"))
+    odd, along = lax.rem(dev, 2), lax.div(dev, 2)
+    here = (1 - odd) * along + odd * (chips - 1 - along)
+
+    def dev_at(position):
+        position = lax.rem(position + chips, chips)
+        back = lax.div(position, half_ring)
+        return (1 - back) * 2 * position + back * (2 * (chips - 1 - position) + 1)
+
+    sibling = (rep, 1 - node, dev)
+    onward = ((rep, node, dev_at(here + 1)), (rep, node, dev_at(here - 1)))
+    expert = lax.div(node * chips + dev, SHARDS)
+
+    def place(way, distance):
+        if distance == 0:
+            return 0
+        if distance == half_ring:
+            return chips - 1
+        return 2 * distance - 1 + way
+
+    def gather_copy(step, way, h):
+        k = (step * 2 + way) * 2 + h
+        return pltpu.make_async_remote_copy(
+            src_ref=tok.at[pl.ds(place(way, step) * 2 * rows + h * half, half), :],
+            dst_ref=tok.at[pl.ds(place(way, step + 1) * 2 * rows + h * half, half), :],
+            send_sem=ag_send.at[k],
+            recv_sem=ag_recv.at[k],
+            device_id=onward[way],
+            device_id_type=MESH,
+        )
+
+    def sibling_copy(spot, h):
+        k = spot * 2 + h
+        return pltpu.make_async_remote_copy(
+            src_ref=tok.at[pl.ds(spot * 2 * rows + h * half, half), :],
+            dst_ref=tok.at[pl.ds(spot * 2 * rows + rows + h * half, half), :],
+            send_sem=sib_send.at[k],
+            recv_sem=sib_recv.at[k],
+            device_id=sibling,
+            device_id_type=MESH,
+        )
+
+    def part_copy(spot):
+        return pltpu.make_async_remote_copy(
+            src_ref=part.at[pl.ds(spot * 2 * rows + rows, rows), :],
+            dst_ref=sib_part.at[pl.ds(spot * rows, rows), :],
+            send_sem=part_send.at[spot],
+            recv_sem=part_recv.at[spot],
+            device_id=sibling,
+            device_id_type=MESH,
+        )
+
+    def scatter_copy(step, way, h):
+        k = (step * 2 + way) * 2 + h
+        return pltpu.make_async_remote_copy(
+            src_ref=sent.at[pl.ds(k * half, half), :],
+            dst_ref=got.at[pl.ds(k * half, half), :],
+            send_sem=rs_send.at[k],
+            recv_sem=rs_recv.at[k],
+            device_id=onward[way],
+            device_id_type=MESH,
+        )
+
+    def crosses(step, way, h):
+        return step < half_ring - 1 or way == h
+
+    loads = [
+        pltpu.make_async_copy(tokens_ref, tok.at[pl.ds(0, rows), pl.ds(0, width)], load_sem.at[0]),
+        pltpu.make_async_copy(gate_ref, w_gate, load_sem.at[1]),
+        pltpu.make_async_copy(up_ref, w_up, load_sem.at[2]),
+        pltpu.make_async_copy(down_ref, w_down, load_sem.at[3]),
+    ]
+    for load in loads:
+        load.start()
+
+    barrier = pltpu.get_barrier_semaphore()
+    for peer in (sibling, onward[CW], onward[CCW]):
+        pl.semaphore_signal(barrier, inc=1, device_id=peer, device_id_type=MESH)
+
+    lane = lax.broadcasted_iota(jnp.int32, (rows, LANES), 1)
+    lane_expert = lax.rem(lane, LANES // 2)
+    dense = jnp.zeros((rows, LANES), jnp.float32)
+    for k in range(picks_ref.shape[1]):
+        dense += jnp.where(picks_ref[:, k : k + 1] == lane_expert, mix_ref[:, k : k + 1], 0.0)
+    high = dense.astype(jnp.bfloat16).astype(jnp.float32)
+    low = dense - high
+    tok[0:rows, width : width + LANES] = jnp.where(lane < LANES // 2, high, low).astype(
+        jnp.bfloat16
+    )
+
+    pl.semaphore_wait(barrier, 3)
+    loads[0].wait()
+
+    started = []
+
+    def start(copy):
+        copy.start()
+        started.append(copy)
+
+    def work(spot, count):
+        first = spot * 2 * rows
+        m = count * 2 * rows
+        x = tok[first : first + m, 0:width]
+        g = jnp.dot(x, w_gate[...], preferred_element_type=jnp.float32)
+        u = jnp.dot(x, w_up[...], preferred_element_type=jnp.float32)
+        hidden = (g / (1.0 + jnp.exp(-g)) * u).astype(jnp.bfloat16)
+        tail = tok[first : first + m, width : width + LANES].astype(jnp.float32)
+        mine = lax.rem(lax.broadcasted_iota(jnp.int32, (m, LANES), 1), LANES // 2) == expert
+        weight = jnp.sum(jnp.where(mine, tail, 0.0), axis=1, keepdims=True)
+        tile = 512
+
+        @pl.loop(0, width // tile)
+        def _(t):
+            cols = pl.ds(pl.multiple_of(t * tile, tile), tile)
+            o = jnp.dot(hidden, w_down[:, cols], preferred_element_type=jnp.float32)
+            part[first : first + m, cols] = (o * weight).astype(jnp.bfloat16)
+
+        for i in range(count):
+            start(part_copy(spot + i))
+
+    def add_up(dst, dst_row, spot, h, extra):
+        a, b = spot * 2 * rows + h * half, spot * rows + h * half
+        tile = 1024
+
+        @pl.loop(0, width // tile)
+        def _(t):
+            cols = pl.ds(pl.multiple_of(t * tile, tile), tile)
+            total = part[a : a + half, cols].astype(jnp.float32)
+            total += sib_part[b : b + half, cols].astype(jnp.float32)
+            for k in extra:
+                total += got[k * half : (k + 1) * half, cols].astype(jnp.float32)
+            dst[dst_row : dst_row + half, cols] = total.astype(jnp.bfloat16)
+
+    for h in (0, 1):
+        for way in (CW, CCW):
+            if crosses(0, way, h):
+                start(gather_copy(0, way, h))
+    for h in (0, 1):
+        start(sibling_copy(0, h))
+    for load in loads[1:]:
+        load.wait()
+    for h in (0, 1):
+        sibling_copy(0, h).wait_recv()
+    work(0, 1)
+    for step in range(1, half_ring):
+        for h in (0, 1):
+            for way in (CW, CCW):
+                gather_copy(step - 1, way, h).wait_recv()
+                if crosses(step, way, h):
+                    start(gather_copy(step, way, h))
+                start(sibling_copy(place(way, step), h))
+        for h in (0, 1):
+            for way in (CW, CCW):
+                sibling_copy(place(way, step), h).wait_recv()
+        work(place(CW, step), 2)
+    for h in (0, 1):
+        gather_copy(half_ring - 1, h, h).wait_recv()
+        start(sibling_copy(chips - 1, h))
+    for h in (0, 1):
+        sibling_copy(chips - 1, h).wait_recv()
+    work(chips - 1, 1)
+
+    part_copy(chips - 1).wait_recv()
+    for h in (0, 1):
+        k = h * 2 + h
+        add_up(sent, k * half, chips - 1, h, ())
+        start(scatter_copy(0, h, h))
+    for step in range(1, half_ring):
+        spots = (place(CCW, half_ring - step), place(CW, half_ring - step))
+        part_copy(spots[0]).wait_recv()
+        part_copy(spots[1]).wait_recv()
+        order = [(CW, 0), (CCW, 0), (CW, 1), (CCW, 1)]
+        if step == 1:
+            order = [(CW, 1), (CCW, 0), (CW, 0), (CCW, 1)]
+        for way, h in order:
+            extra = ()
+            if step > 1 or way == h:
+                scatter_copy(step - 1, way, h).wait_recv()
+                extra = (((step - 1) * 2 + way) * 2 + h,)
+            k = (step * 2 + way) * 2 + h
+            add_up(sent, k * half, spots[way], h, extra)
+            start(scatter_copy(step, way, h))
+    part_copy(0).wait_recv()
+    for h in (0, 1):
+        extra = []
+        for way in (CW, CCW):
+            scatter_copy(half_ring - 1, way, h).wait_recv()
+            extra.append(((half_ring - 1) * 2 + way) * 2 + h)
+        add_up(out_ref, h * half, 0, h, tuple(extra))
+    for copy in started:
+        copy.wait_send()
+
+
+def on_ring(tokens, expert_picks, mix_weights, w_gate, w_up, w_down):
+    rows, width = tokens.shape
+    chips = lax.axis_size("dev")
+    ff = w_gate.shape[1]
+    wide = width + LANES
+    dma = pltpu.SemaphoreType.DMA
+    vmem = pl.BlockSpec(memory_space=pltpu.VMEM)
+    hbm = pl.BlockSpec(memory_space=pl.ANY)
+    bf16 = jnp.bfloat16
+    return pl.pallas_call(
+        functools.partial(ring_kernel, chips, rows, width),
+        out_shape=jax.ShapeDtypeStruct((rows, width), bf16),
+        in_specs=[vmem, vmem, hbm, hbm, hbm, hbm],
+        out_specs=vmem,
+        scratch_shapes=[
+            pltpu.VMEM((2 * chips * rows, wide), bf16),
+            pltpu.VMEM((width, ff), bf16),
+            pltpu.VMEM((width, ff), bf16),
+            pltpu.VMEM((ff, width), bf16),
+            pltpu.VMEM((2 * chips * rows, width), bf16),
+            pltpu.VMEM((chips * rows, width), bf16),
+            pltpu.VMEM((chips * rows, width), bf16),
+            pltpu.VMEM((chips * rows, width), bf16),
+            dma((4,)),
+            dma((2 * chips,)),
+            dma((2 * chips,)),
+            dma((2 * chips,)),
+            dma((2 * chips,)),
+            dma((chips,)),
+            dma((chips,)),
+            dma((2 * chips,)),
+            dma((2 * chips,)),
+        ],
+        compiler_params=pltpu.CompilerParams(
+            collective_id=0, has_side_effects=True, vmem_limit_bytes=58 * 2**20
+        ),
+        cost_estimate=pl.CostEstimate(
+            flops=2 * 2 * chips * rows * width * ff * 3,
+            bytes_accessed=3 * 2 * width * ff,
+            transcendentals=2 * chips * rows * ff,
+        ),
+    )(expert_picks, mix_weights, tokens, w_gate, w_up, w_down)
+
+
+def on_slots(tokens, expert_picks, mix_weights, w_gate, w_up, w_down):
     rows_here = tokens.shape[0]
     model_width = tokens.shape[1]
     pick_count = expert_picks.shape[1]
@@ -63,8 +338,10 @@
         P(None, ("node", "dev")),
         P(("node", "dev"), None),
     )
+    sources = mesh.shape["node"] * mesh.shape["dev"]
+    few = sources // SHARDS <= 4 and mesh.shape["node"] == 2 and mesh.shape["dev"] % 4 == 0
     return jax.shard_map(
-        on_device,
+        on_ring if few else on_slots,
         mesh=mesh,
         in_specs=placed,
         out_specs=P(("rep", "node", "dev"), None),

time: 373 us -> 95.3 us (0.26); the launches traced: 366 us -> 94.9 us
  blocking collectives: 169 us -> 0 us
  waiting for transfers between devices: 153 us -> 0 us
  Pallas kernels: 0 us -> 90.4 us
  matrix products: 18.1 us -> 0 us
  other arithmetic: 8.85 us -> 0 us
  local copies, waits for them, and re-layouts: 11.6 us -> 4.54 us
  starting transfers between devices: 4.99 us -> 0 us
    all_to_all x1 -> x0, blocking collectives: 169 us -> none  [on_device(): lax.all_to_all(spread, ('node', 'dev'), split_axis=0, concat_axis=0, tile...]
    all_to_all x1 -> x0, waiting for transfers between devices: 153 us -> none  [on_device(): lax.all_to_all(shard_out.reshape(leading, row_count, model_width), ('node...]
    pallas_call x0 -> x1, Pallas kernels: none -> 90.4 us  [on_ring(): pl.pallas_call(functools.partial(ring_kernel, chips, rows, width), out_sh...]
    dot_general x2 -> x0, matrix products: 18.1 us -> none  [the longest x1 16 us: on_device(): jnp.dot(hidden, w_down, preferred_element_type=jnp.float32)]
    reduce_sum x3 -> x0, other arithmetic: 7.98 us -> none  [the longest x1 4.61 us: on_device(): jnp.sum(returned.reshape(experts, SHARDS, capacity, model_width).astype(j...]
    all_to_all x1 -> x0, starting transfers between devices: 4.99 us -> none  [on_device(): lax.all_to_all(shard_out.reshape(leading, row_count, model_width), ('node...]
  transfers between devices with their start and end apart: 1 -> 0, of which waited for: 1 -> 0; matrix products, arithmetic and copies ran while one was open for 0% -> 0% of each run, Pallas kernels for 0% -> 0%
where the time goes in v1:
time: 95.3 us; the launch traced here: 94.9 us
  Pallas kernels  90.4 us (95%)
  local copies, waits for them, and re-layouts  4.54 us (5%)
    pallas_call x1, Pallas kernels, on_ring(): pl.pallas_call(functools.partial(ring_kernel, chips, rows, width), out_sh...  90.4 us
    unnamed x3, local copies, waits for them, and re-layouts  4.54 us

profile of v1, /device:TPU:0, one launch (start us, length us, event | category | flops | bytes accessed | tf_op | source)
XLA Modules:
  0.0 94.9 jit_solution(10387260741592948631)
XLA Ops:
  0.0 1.4 %copy.7.picks_ref = s32[32,2]{1,0:T(8,128)} copy(s32[32,2]{0,1:T(2,128)} %param.7) | data formatting | bytes 512 | tf_op args[1]
  1.4 1.4 %copy.8.mix_ref = f32[32,2]{1,0:T(8,128)} copy(f32[32,2]{0,1:T(2,128)} %param.8) | data formatting | bytes 512 | tf_op args[2]
  2.7 90.4 %shard_map.64 = bf16[32,7168]{1,0:T(8,128)(2,1)} custom-call(s32[32,2]{1,0:T(8,128)} %copy.7.picks_ref, f32[32,2]{1,0:T(8,128)} %copy.8.mix_ref, bf16[32,7168]{1,0:T(8,128)(2,1)} %tokens_ref.1, bf16[7168,256]{1,0:T(8,128)(2,1)} %gate_ref.1, bf16[7168,256]{1,0:T(8,128)(2,1)} %up_ref.1, bf16[256,7168]{1,0:T(8,128)(2,1)} %down_ref.1), custom_call_target="tpu_custom_call" | custom-call | flops 5637144576 | bytes 11010048 | tf_op jit(solution)/shard_map/pallas_call | solution.py:249
  93.1 1.8 %copy.10 = bf16[32,7168]{1,0:T(8,128)(2,1)} copy(bf16[32,7168]{1,0:T(8,128)(2,1)} %shard_map.64) | data formatting | bytes 917504

commit v2 on v1

--- a/solution.py
+++ b/solution.py
@@ -11,6 +11,8 @@
 LANES = 128
 MESH = pl.DeviceIdType.MESH
 CW, CCW = 0, 1
+LONG = ((CW, 0), (CCW, 1))
+SHORT = ((CW, 1), (CCW, 0))
 
 
 def ring_kernel(
@@ -123,16 +125,15 @@
     for peer in (sibling, onward[CW], onward[CCW]):
         pl.semaphore_signal(barrier, inc=1, device_id=peer, device_id_type=MESH)
 
-    lane = lax.broadcasted_iota(jnp.int32, (rows, LANES), 1)
-    lane_expert = lax.rem(lane, LANES // 2)
-    dense = jnp.zeros((rows, LANES), jnp.float32)
-    for k in range(picks_ref.shape[1]):
-        dense += jnp.where(picks_ref[:, k : k + 1] == lane_expert, mix_ref[:, k : k + 1], 0.0)
+    line = lax.broadcasted_iota(jnp.int32, (LANES, rows), 0)
+    line_expert = lax.rem(line, LANES // 2)
+    dense = jnp.zeros((LANES, rows), jnp.float32)
+    for k in range(picks_ref.shape[0]):
+        dense += jnp.where(picks_ref[k : k + 1, :] == line_expert, mix_ref[k : k + 1, :], 0.0)
     high = dense.astype(jnp.bfloat16).astype(jnp.float32)
     low = dense - high
-    tok[0:rows, width : width + LANES] = jnp.where(lane < LANES // 2, high, low).astype(
-        jnp.bfloat16
-    )
+    both = jnp.where(line < LANES // 2, high, low)
+    tok[0:rows, width : width + LANES] = both.T.astype(jnp.bfloat16)
 
     pl.semaphore_wait(barrier, 3)
     loads[0].wait()
@@ -177,55 +178,57 @@
                 total += got[k * half : (k + 1) * half, cols].astype(jnp.float32)
             dst[dst_row : dst_row + half, cols] = total.astype(jnp.bfloat16)
 
-    for h in (0, 1):
-        for way in (CW, CCW):
-            if crosses(0, way, h):
-                start(gather_copy(0, way, h))
-    for h in (0, 1):
-        start(sibling_copy(0, h))
-    for load in loads[1:]:
-        load.wait()
-    for h in (0, 1):
-        sibling_copy(0, h).wait_recv()
-    work(0, 1)
-    for step in range(1, half_ring):
-        for h in (0, 1):
-            for way in (CW, CCW):
-                gather_copy(step - 1, way, h).wait_recv()
-                if crosses(step, way, h):
-                    start(gather_copy(step, way, h))
-                start(sibling_copy(place(way, step), h))
-        for h in (0, 1):
-            for way in (CW, CCW):
-                sibling_copy(place(way, step), h).wait_recv()
-        work(place(CW, step), 2)
-    for h in (0, 1):
-        gather_copy(half_ring - 1, h, h).wait_recv()
-        start(sibling_copy(chips - 1, h))
-    for h in (0, 1):
-        sibling_copy(chips - 1, h).wait_recv()
-    work(chips - 1, 1)
-
-    part_copy(chips - 1).wait_recv()
-    for h in (0, 1):
-        k = h * 2 + h
-        add_up(sent, k * half, chips - 1, h, ())
-        start(scatter_copy(0, h, h))
-    for step in range(1, half_ring):
-        spots = (place(CCW, half_ring - step), place(CW, half_ring - step))
-        part_copy(spots[0]).wait_recv()
-        part_copy(spots[1]).wait_recv()
-        order = [(CW, 0), (CCW, 0), (CW, 1), (CCW, 1)]
-        if step == 1:
-            order = [(CW, 1), (CCW, 0), (CW, 0), (CCW, 1)]
-        for way, h in order:
+    def pass_on(step, chain):
+        for way, h in chain:
+            spot = place(1 - way, half_ring - step)
+            if chain is SHORT:
+                part_copy(spot).wait_recv()
             extra = ()
             if step > 1 or way == h:
                 scatter_copy(step - 1, way, h).wait_recv()
                 extra = (((step - 1) * 2 + way) * 2 + h,)
             k = (step * 2 + way) * 2 + h
-            add_up(sent, k * half, spots[way], h, extra)
+            add_up(sent, k * half, spot, h, extra)
             start(scatter_copy(step, way, h))
+
+    for way, h in LONG + SHORT:
+        if crosses(0, way, h):
+            start(gather_copy(0, way, h))
+    for h in (0, 1):
+        start(sibling_copy(0, h))
+    for load in loads[1:]:
+        load.wait()
+    for h in (0, 1):
+        sibling_copy(0, h).wait_recv()
+    work(0, 1)
+    for step in range(1, half_ring):
+        for way, h in LONG + SHORT:
+            gather_copy(step - 1, way, h).wait_recv()
+            if crosses(step, way, h):
+                start(gather_copy(step, way, h))
+            start(sibling_copy(place(way, step), h))
+        for h in (0, 1):
+            for way in (CW, CCW):
+                sibling_copy(place(way, step), h).wait_recv()
+        work(place(CW, step), 2)
+    for way, h in LONG:
+        gather_copy(half_ring - 1, way, h).wait_recv()
+        start(sibling_copy(chips - 1, h))
+    pass_on(1, SHORT)
+    for h in (0, 1):
+        sibling_copy(chips - 1, h).wait_recv()
+    work(chips - 1, 1)
+
+    if half_ring > 2:
+        pass_on(2, SHORT)
+    part_copy(chips - 1).wait_recv()
+    for h in (0, 1):
+        add_up(sent, (h * 2 + h) * half, chips - 1, h, ())
+        start(scatter_copy(0, h, h))
+    for step in range(1, half_ring):
+        pass_on(step, LONG)
+        if step + 2 < half_ring:
+            pass_on(step + 2, SHORT)
     part_copy(0).wait_recv()
     for h in (0, 1):
         extra = []
@@ -278,7 +281,7 @@
             bytes_accessed=3 * 2 * width * ff,
             transcendentals=2 * chips * rows * ff,
         ),
-    )(expert_picks, mix_weights, tokens, w_gate, w_up, w_down)
+    )(expert_picks.T, mix_weights.T, tokens, w_gate, w_up, w_down)
 
 
 def on_slots(tokens, expert_picks, mix_weights, w_gate, w_up, w_down):

time: 95.3 us -> 86.3 us (0.906)
  Pallas kernels: 90.4 us -> 84.3 us
  local copies, waits for them, and re-layouts: 4.54 us -> 1.82 us
    pallas_call x1, Pallas kernels: 90.4 us -> 84.3 us  [on_ring(): pl.pallas_call(functools.partial(ring_kernel, chips, rows, width), out_sh...]
    unnamed x3 -> x1, local copies, waits for them, and re-layouts: 4.54 us -> 1.82 us
where the time goes in v2:
time: 86.3 us; the launch traced here: 86.2 us
  Pallas kernels  84.3 us (98%)
  local copies, waits for them, and re-layouts  1.82 us (2%)
    pallas_call x1, Pallas kernels, on_ring(): pl.pallas_call(functools.partial(ring_kernel, chips, rows, width), out_sh...  84.3 us
    unnamed x1, local copies, waits for them, and re-layouts  1.82 us

profile of v2, /device:TPU:0, one launch (start us, length us, event | category | flops | bytes accessed | tf_op | source)
XLA Modules:
  0.0 86.2 jit_solution(7463714622676333645)
XLA Ops:
  0.0 84.3 %shard_map.64 = bf16[32,7168]{1,0:T(8,128)(2,1)} custom-call(s32[2,32]{1,0:T(2,128)} %bitcast.2, f32[2,32]{1,0:T(2,128)} %bitcast.3, bf16[32,7168]{1,0:T(8,128)(2,1)} %tokens_ref.1, bf16[7168,256]{1,0:T(8,128)(2,1)} %gate_ref.1, bf16[7168,256]{1,0:T(8,128)(2,1)} %up_ref.1, bf16[256,7168]{1,0:T(8,128)(2,1)} %down_ref.1), custom_call_target="tpu_custom_call" | custom-call | flops 5637144576 | bytes 11010048 | tf_op jit(solution)/shard_map/pallas_call | solution.py:252
  84.3 1.8 %copy.8 = bf16[32,7168]{1,0:T(8,128)(2,1)} copy(bf16[32,7168]{1,0:T(8,128)(2,1)} %shard_map.64) | data formatting | bytes 917504
